TPU v7x, 32 devices: a whole 2x2x4 slice. The times are simulated.
32 devices in a mesh: outer: 8 (over z, y), inner: 4 (over x, core).
Axes of the slice: x: 2, y: 2, z: 4, core: 2. Of those that a mesh axis runs over, the one named last changes fastest.
Arguments:
- hidden_in: bfloat16 [65536, 1024], P(('outer', 'inner')), may hold values from -6 to 6
- segment_ids: int32 [65536], P(('outer', 'inner')), may hold values from 0 to 15, never falling along the last dimension, each value on 1 to 16384 neighbouring positions
- query_weight: bfloat16 [1024, 1024], replicated, may hold values from -0.1875 to 0.1875
- key_weight: bfloat16 [1024, 1024], replicated, may hold values from -0.1875 to 0.1875
- value_weight: bfloat16 [1024, 1024], replicated, may hold values from -0.1875 to 0.1875
- output_weight: bfloat16 [1024, 1024], replicated, may hold values from -0.1875 to 0.1875
- head_gain: float32 [1024], replicated, may hold values from 0.1 to 1.9
Outputs:
- layer_out: bfloat16 [65536, 1024], P(('outer', 'inner'))
Inputs may be any that keep to these rules, and one draw needn't show every extreme that they name: `segment_ids`: ids never fall along the window; each history spans 1 to 16384 tokens and one spans exactly 16384.
All inputs are finite; a program needn't handle non-finite values.
Results may differ from a plain program's by a relative error of at most 0.011.
Values sent between devices are 32-bit elements; how exact they have to be, the bound alone decides.
A program may use at most 256 MiB of HBM per device.

v0:
```python
import jax
import jax.numpy as jnp
from jax import lax
from jax.sharding import PartitionSpec as P

D = 1024
H = 8
HD = 128
BLK = 512


def from_behind(x, axis, by):
    size = lax.axis_size(axis)
    pairs = [(i, i + by) for i in range(size) if 0 <= i + by < size]
    return lax.ppermute(x, axis, pairs)


def combine(early, late):
    state_e, first_e, last_e, clean_e = early
    state_l, first_l, last_l, clean_l = late
    joined = (last_e == first_l) | (last_e < 0) | (first_l < 0)
    take = (clean_l > 0) & ((first_l == last_e) | (first_l < 0))
    state = state_l + jnp.where(take, state_e, jnp.zeros_like(state_e))
    first = jnp.where(first_e < 0, first_l, first_e)
    last = jnp.where(last_l < 0, last_e, last_l)
    clean = clean_e * clean_l * joined.astype(jnp.int32)
    return (state, first, last, clean)


def state_product(form, queries, state):
    high_part = state.astype(jnp.bfloat16)
    low_part = (state - high_part.astype(jnp.float32)).astype(jnp.bfloat16)
    first_term = jnp.einsum(form, queries, high_part, preferred_element_type=jnp.float32)
    return first_term + jnp.einsum(form, queries, low_part, preferred_element_type=jnp.float32)


def local_pass(queries, keys, values, segment_ids):
    tokens = queries.shape[0]
    blocks = tokens // BLK
    q_blocks = queries.reshape(blocks, BLK, H, HD)
    k_blocks = keys.reshape(blocks, BLK, H, HD)
    v_blocks = values.reshape(blocks, BLK, H, HD)
    id_blocks = segment_ids.reshape(blocks, BLK)
    causal = jnp.tril(jnp.ones((BLK, BLK), dtype=bool))

    def step(carry, block):
        state, last_id = carry
        q_b, k_b, v_b, i_b = block
        keep = causal & (i_b[:, None] == i_b[None, :])
        scores = jnp.einsum("shd,thd->hst", q_b, k_b, preferred_element_type=jnp.float32)
        scores = jnp.where(keep[None], scores, 0.0).astype(jnp.bfloat16)
        local = jnp.einsum("hst,thd->shd", scores, v_b, preferred_element_type=jnp.float32)
        carried = state_product("shd,hde->she", q_b, state)
        carried = carried * (i_b == last_id).astype(jnp.float32)[:, None, None]
        tail = (i_b == i_b[-1]).astype(jnp.bfloat16)[:, None, None]
        contrib = jnp.einsum("thd,the->hde", k_b * tail, v_b, preferred_element_type=jnp.float32)
        held = (i_b[0] == i_b[-1]) & (i_b[0] == last_id)
        state = jnp.where(held, state, jnp.zeros_like(state)) + contrib
        return ((state, i_b[-1]), local + carried)

    init = (jnp.zeros((H, HD, HD), jnp.float32), jnp.array(-1, dtype=jnp.int32))
    (final_state, _), mixed = lax.scan(step, init, (q_blocks, k_blocks, v_blocks, id_blocks))
    return (mixed.reshape(tokens, H, HD), final_state)


def body(hidden_in, segment_ids, query_weight, key_weight, value_weight, output_weight, head_gain):
    tokens = hidden_in.shape[0]
    queries = jnp.dot(hidden_in, query_weight, preferred_element_type=jnp.float32).astype(
        jnp.bfloat16
    )
    keys = jnp.dot(hidden_in, key_weight, preferred_element_type=jnp.float32).astype(jnp.bfloat16)
    values = jnp.dot(hidden_in, value_weight, preferred_element_type=jnp.float32).astype(
        jnp.bfloat16
    )
    mixed, trailing = local_pass(
        queries.reshape(tokens, H, HD),
        keys.reshape(tokens, H, HD),
        values.reshape(tokens, H, HD),
        segment_ids,
    )
    first_id = segment_ids[0]
    last_id = segment_ids[-1]
    clean = (first_id == last_id).astype(jnp.int32)
    summary = (trailing, first_id, last_id, clean)
    neutral = (
        jnp.zeros_like(trailing),
        jnp.array(-1, dtype=jnp.int32),
        jnp.array(-1, dtype=jnp.int32),
        jnp.array(1, dtype=jnp.int32),
    )
    position = lax.axis_index(("outer", "inner"))
    running = summary
    for turn, distance in enumerate((1, 1, 2, 4)):
        moved = from_behind(
            (running[0], running[1], running[2], running[3]), ("outer", "inner"), distance
        )
        valid = position >= distance
        moved = jax.tree.map(lambda got, empty: jnp.where(valid, got, empty), tuple(moved), neutral)
        running = moved if turn == 0 else combine(moved, running)
    carry_state, _, carry_last, _ = running
    extra = state_product("thd,hde->the", queries.reshape(tokens, H, HD), carry_state)
    mixed = mixed + extra * (segment_ids == carry_last).astype(jnp.float32)[:, None, None]
    scale = lax.rsqrt(jnp.mean(mixed * mixed, axis=-1, keepdims=True) + 1e-06)
    normed = (mixed * scale * head_gain.reshape(H, HD)).astype(jnp.bfloat16).reshape(tokens, D)
    return jnp.dot(normed, output_weight, preferred_element_type=jnp.float32).astype(jnp.bfloat16)


def solution(mesh):
    in_specs = (P(("outer", "inner"), None), P(("outer", "inner")), P(), P(), P(), P(), P())
    out_specs = P(("outer", "inner"), None)
    return jax.shard_map(body, mesh=mesh, in_specs=in_specs, out_specs=out_specs, check_vma=False)
```

profile of v0, /device:TPU:8, one launch (start us, length us, event | category | flops | bytes accessed | tf_op | source)
XLA Modules:
  0.0 420.1 jit_solution(15518817049716609124)
XLA Ops:
  1.6 6.9 %convert_bitcast_fusion.1 = bf16[256,8,8,128]{3,1,2,0:T(8,128)(2,1)S(1)} fusion(bf16[2048,1024]{1,0:T(8,128)(2,1)} %param.9, bf16[1024,1024]{1,0:T(8,128)(2,1)S(1)} %copy-done), kind=kOutput, calls=%fused_computation.47 | convolution fusion | flops 4297064448 | bytes 10485760 | tf_op jit(solution)/shard_map/dot_general | solution.py:71
  8.6 3.3 copy.31
  11.8 1.1 copy-done.6
  12.9 4.7 %convert_bitcast_fusion = bf16[256,8,8,128]{3,1,2,0:T(8,128)(2,1)S(1)} fusion(bf16[2048,1024]{1,0:T(8,128)(2,1)S(1)} %copy-done.5, bf16[1024,1024]{1,0:T(8,128)(2,1)S(1)} %copy-done.6), kind=kOutput, calls=%fused_computation.46 | convolution fusion | flops 4297064448 | bytes 10485760 | tf_op jit(solution)/shard_map/dot_general | solution.py:72
  17.6 3.1 copy.32
  20.7 6.1 %convolution_convert_fusion.1 = bf16[2048,1024]{0,1:T(8,128)(2,1)} fusion(bf16[2048,1024]{1,0:T(8,128)(2,1)S(1)} %copy-done.5, bf16[1024,1024]{1,0:T(8,128)(2,1)S(1)} %copy-done.7), kind=kOutput, calls=%fused_computation.49 | convolution fusion | flops 4297064448 | bytes 10485760 | tf_op jit(solution)/shard_map/dot_general | solution.py:68
  26.9 7.9 %reshape_reshape.11 = bf16[4,512,8,128]{1,0,3,2:T(4,128)(2,1)} reshape(bf16[2048,1024]{0,1:T(8,128)(2,1)} %convolution_convert_fusion.1) | data formatting | bytes 8388608 | tf_op jit(solution)/shard_map/reshape;reshape | solution.py:40
  34.8 7.9 %copy.13 = bf16[4,512,8,128]{3,1,2,0:T(8,128)(2,1)} copy(bf16[4,512,8,128]{1,0,3,2:T(4,128)(2,1)} %reshape_reshape.11) | data formatting | bytes 8388608
  42.7 267.0 %while.15 = (s32[]{:T(128)}, f32[8,128,128]{2,1,0:T(8,128)S(1)}, s32[]{:T(128)}, f32[4,512,8,128]{1,0,3,2:T(4,128)}, s32[4,512]{1,0:T(4,128)S(1)}, /*index=5*/bf...) while((s32[]{:T(128)}, f32[8,128,128]{2,1,0:T(8,128)S(1)}, ...), condition=%wide.region_1.2_spmd.clone, body=%wide.region_0.1_spmd.clone.sunk | while | flops 1484654592 | bytes 35141856 | solution.py:62
  42.7 3.1 fusion.65
  45.8 3.1 fusion.64
  48.9 1.7 constant_dynamic-slice_fusion.7
  50.6 1.5 copy.42
  55.3 1.7 convolution_add_fusion.2
  57.2 6.9 %fusion.67 = f32[1,512,8,128]{1,3,2,0:T(8,128)} fusion(f32[8,128,512]{2,1,0:T(8,128)} %fusion.64, f32[8,512,128]{1,2,0:T(8,128)} %fusion.65, pred[512,512]{1,0:T(8,128)(4,1)S(1)} %fusion.66, bf16[1,512,8,128]{1,3,2,0:T(8,128)(2,1)} %copy.42, f32[512]{0:T(512)S(1)} %get-tuple-element.178, bf16[1,512,8,128]{3,2,1,0:T(8,128)(2,1)S(1)} %get-tuple-element.174, ...), kind=kOutput, calls=%fused_computation.9.clone.1 | convolution fusion | flops 1079508992 | bytes 9701380 | tf_op jit(solution)/shard_map/while/body/eval_jaxpr/hst,thd->shd/dot_general | solution.py:52
  64.2 3.8 copy.43
  67.9 40.8 %dynamic_update_slice.6 = f32[4,512,8,128]{1,0,3,2:T(4,128)} dynamic-update-slice(f32[4,512,8,128]{1,0,3,2:T(4,128)} %get-tuple-element.193, f32[1,512,8,128]{1,0,3,2:T(1,128)S(1)} %copy.43, s32[]{:T(128)S(6)} %copy.49, s32[]{:T(128)} %constant.19.clone.1..sunk, s32[]{:T(128)} %constant.19.clone.1..sunk, s32[]{:T(128)} %constant.19.clone.1..sunk) | dynamic-update-slice | bytes 4194308 | tf_op jit(solution)/shard_map/while/body/jit(dynamic_update_index_in_dim)/dynamic_update_slice | solution.py:62
  109.5 3.1 fusion.65
  112.5 3.1 fusion.64
  115.6 1.7 constant_dynamic-slice_fusion.7
  117.3 1.5 copy.42
  122.0 1.7 convolution_add_fusion.2
  124.0 6.9 %fusion.67 = f32[1,512,8,128]{1,3,2,0:T(8,128)} fusion(f32[8,128,512]{2,1,0:T(8,128)} %fusion.64, f32[8,512,128]{1,2,0:T(8,128)} %fusion.65, pred[512,512]{1,0:T(8,128)(4,1)S(1)} %fusion.66, bf16[1,512,8,128]{1,3,2,0:T(8,128)(2,1)} %copy.42, f32[512]{0:T(512)S(1)} %get-tuple-element.178, bf16[1,512,8,128]{3,2,1,0:T(8,128)(2,1)S(1)} %get-tuple-element.174, ...), kind=kOutput, calls=%fused_computation.9.clone.1 | convolution fusion | flops 1079508992 | bytes 9701380 | tf_op jit(solution)/shard_map/while/body/eval_jaxpr/hst,thd->shd/dot_general | solution.py:52
  130.9 3.8 copy.43
  134.7 40.8 %dynamic_update_slice.6 = f32[4,512,8,128]{1,0,3,2:T(4,128)} dynamic-update-slice(f32[4,512,8,128]{1,0,3,2:T(4,128)} %get-tuple-element.193, f32[1,512,8,128]{1,0,3,2:T(1,128)S(1)} %copy.43, s32[]{:T(128)S(6)} %copy.49, s32[]{:T(128)} %constant.19.clone.1..sunk, s32[]{:T(128)} %constant.19.clone.1..sunk, s32[]{:T(128)} %constant.19.clone.1..sunk) | dynamic-update-slice | bytes 4194308 | tf_op jit(solution)/shard_map/while/body/jit(dynamic_update_index_in_dim)/dynamic_update_slice | solution.py:62
  176.2 3.1 fusion.65
  179.3 3.1 fusion.64
  182.4 1.7 constant_dynamic-slice_fusion.7
  184.1 1.5 copy.42
  188.8 1.7 convolution_add_fusion.2
  190.7 6.9 %fusion.67 = f32[1,512,8,128]{1,3,2,0:T(8,128)} fusion(f32[8,128,512]{2,1,0:T(8,128)} %fusion.64, f32[8,512,128]{1,2,0:T(8,128)} %fusion.65, pred[512,512]{1,0:T(8,128)(4,1)S(1)} %fusion.66, bf16[1,512,8,128]{1,3,2,0:T(8,128)(2,1)} %copy.42, f32[512]{0:T(512)S(1)} %get-tuple-element.178, bf16[1,512,8,128]{3,2,1,0:T(8,128)(2,1)S(1)} %get-tuple-element.174, ...), kind=kOutput, calls=%fused_computation.9.clone.1 | convolution fusion | flops 1079508992 | bytes 9701380 | tf_op jit(solution)/shard_map/while/body/eval_jaxpr/hst,thd->shd/dot_general | solution.py:52
  197.7 3.8 copy.43
  201.4 40.8 %dynamic_update_slice.6 = f32[4,512,8,128]{1,0,3,2:T(4,128)} dynamic-update-slice(f32[4,512,8,128]{1,0,3,2:T(4,128)} %get-tuple-element.193, f32[1,512,8,128]{1,0,3,2:T(1,128)S(1)} %copy.43, s32[]{:T(128)S(6)} %copy.49, s32[]{:T(128)} %constant.19.clone.1..sunk, s32[]{:T(128)} %constant.19.clone.1..sunk, s32[]{:T(128)} %constant.19.clone.1..sunk) | dynamic-update-slice | bytes 4194308 | tf_op jit(solution)/shard_map/while/body/jit(dynamic_update_index_in_dim)/dynamic_update_slice | solution.py:62
  243.0 3.1 fusion.65
  246.0 3.1 fusion.64
  249.1 1.7 constant_dynamic-slice_fusion.7
  250.8 1.5 copy.42
  255.6 1.7 convolution_add_fusion.2
  257.5 6.9 %fusion.67 = f32[1,512,8,128]{1,3,2,0:T(8,128)} fusion(f32[8,128,512]{2,1,0:T(8,128)} %fusion.64, f32[8,512,128]{1,2,0:T(8,128)} %fusion.65, pred[512,512]{1,0:T(8,128)(4,1)S(1)} %fusion.66, bf16[1,512,8,128]{1,3,2,0:T(8,128)(2,1)} %copy.42, f32[512]{0:T(512)S(1)} %get-tuple-element.178, bf16[1,512,8,128]{3,2,1,0:T(8,128)(2,1)S(1)} %get-tuple-element.174, ...), kind=kOutput, calls=%fused_computation.9.clone.1 | convolution fusion | flops 1079508992 | bytes 9701380 | tf_op jit(solution)/shard_map/while/body/eval_jaxpr/hst,thd->shd/dot_general | solution.py:52
  264.4 3.8 copy.43
  268.2 40.8 %dynamic_update_slice.6 = f32[4,512,8,128]{1,0,3,2:T(4,128)} dynamic-update-slice(f32[4,512,8,128]{1,0,3,2:T(4,128)} %get-tuple-element.193, f32[1,512,8,128]{1,0,3,2:T(1,128)S(1)} %copy.43, s32[]{:T(128)S(6)} %copy.49, s32[]{:T(128)} %constant.19.clone.1..sunk, s32[]{:T(128)} %constant.19.clone.1..sunk, s32[]{:T(128)} %constant.19.clone.1..sunk) | dynamic-update-slice | bytes 4194308 | tf_op jit(solution)/shard_map/while/body/jit(dynamic_update_index_in_dim)/dynamic_update_slice | solution.py:62
  309.7 1.9 collective-permute-start
  311.6 10.4 %collective-permute-done = f32[8,128,128]{2,1,0:T(8,128)S(1)} collective-permute-done((f32[8,128,128]{2,1,0:T(8,128)S(1)}, f32[8,128,128]{2,1,0:T(8,128)S(1)}, u32[]{:S(2)}, u32[]{:S(2)}) %collective-permute-start) | collective-permute-done | bytes 524320 | tf_op jit(solution)/shard_map/ppermute | solution.py:15
  322.0 1.9 collective-permute-start.5
  324.6 1.9 collective-permute-start.3
  326.5 1.9 collective-permute-start.2
  329.8 5.0 %collective-permute-start.1 = (s32[]{:T(128)}, s32[]{:T(128)}, u32[]{:S(2)}, u32[]{:S(2)}) collective-permute-start(s32[]{:T(128)} %convert_element_type.61), channel_id=1, source_target_pairs={{0,1},{1,2},{2,3},{3,4},{4,5},{5,6},{6,7},{7,8},{8,9},{9,10},{10,1... | collective-permute-start | bytes 20 | tf_op jit(solution)/shard_map/ppermute | solution.py:15
  335.4 2.9 collective-permute-start.4
  339.6 2.6 collective-permute-done.4
  342.9 1.9 collective-permute-start.9
  344.9 3.8 collective-permute-start.6
  348.6 11.5 %collective-permute-start.7 = (s32[]{:T(128)}, s32[]{:T(128)}, u32[]{:S(2)}, u32[]{:S(2)}) collective-permute-start(s32[]{:T(128)} %select_n.103), channel_id=1, source_target_pairs={{0,1},{1,2},{2,3},{3,4},{4,5},{5,6},{6,7},{7,8},{8,9},{9,10},{10,1... | collective-permute-start | bytes 20 | tf_op jit(solution)/shard_map/ppermute | solution.py:15
  360.1 3.2 collective-permute-start.8
  364.6 2.7 collective-permute-done.8
  368.1 1.9 collective-permute-start.13
  370.0 10.9 %reshape.73 = f32[2048,8,128]{0,2,1:T(8,128)} reshape(f32[4,512,8,128]{1,0,3,2:T(4,128)} %get-tuple-element.53) | data formatting | bytes 16777216 | tf_op jit(solution)/shard_map/reshape | solution.py:63
  380.9 5.0 %collective-permute-start.10 = (s32[]{:T(128)}, s32[]{:T(128)}, u32[]{:S(2)}, u32[]{:S(2)}) collective-permute-start(s32[]{:T(128)} %mul.65), channel_id=1, source_target_pairs={{0,2},{1,3},{2,4},{3,5},{4,6},{5,7},{6,8},{7,9},{8,10},{9,11},{10,... | collective-permute-start | bytes 20 | tf_op jit(solution)/shard_map/ppermute | solution.py:15
  385.9 5.9 %collective-permute-start.11 = (s32[]{:T(128)}, s32[]{:T(128)}, u32[]{:S(2)}, u32[]{:S(2)}) collective-permute-start(s32[]{:T(128)} %select_n.111), channel_id=1, source_target_pairs={{0,2},{1,3},{2,4},{3,5},{4,6},{5,7},{6,8},{7,9},{8,10},{9,11},{10,... | collective-permute-start | bytes 20 | tf_op jit(solution)/shard_map/ppermute | solution.py:15
  391.7 3.2 collective-permute-start.12
  396.3 1.8 collective-permute-done.12
  398.8 3.6 fusion.35
  402.4 7.0 %multiply_reduce_fusion = (f32[2048,8]{0,1:T(8,128)S(1)}, f32[2048,8,128]{0,2,1:T(8,128)}) fusion(f32[2048,8,128]{0,2,1:T(8,128)} %reshape.73, f32[2048]{0:T(1024)S(1)} %compare_convert_fusion.2, f32[8,128,2048]{2,1,0:T(8,128)S(1)} %fusion.35, bf16[2048,8,128]{0,2,1:T(8,128)(2,1)S(1)} %bitcast.93, f32[8,128,128]{2,1,0:T(8,128)S(1)} %select_add_fusion.1, ...), kind=kOutput, calls=%fused_computation.45 | convolution fusion | flops 547864576 | bytes 30482434 | tf_op jit(solution)/shard_map/thd,hde->the/dot_general | solution.py:33
  409.5 4.4 %multiply_convert_fusion = bf16[2048,8,128]{0,2,1:T(8,128)(2,1)S(1)} fusion(f32[2048,8,128]{0,2,1:T(8,128)} %get-tuple-element.117, f32[8,128]{1,0:T(8,128)S(1)} %bitcast.99, f32[2048,8]{0,1:T(8,128)S(1)} %add_rsqrt_fusion), kind=kLoop, calls=%fused_computation.44 | loop fusion | flops 6291456 | bytes 12652544 | tf_op jit(solution)/shard_map/convert_element_type | solution.py:104
  413.9 6.2 %convolution_convert_fusion = bf16[2048,1024]{1,0:T(8,128)(2,1)} fusion(bf16[2048,1024]{0,1:T(8,128)(2,1)S(1)} %bitcast.96, bf16[1024,1024]{1,0:T(8,128)(2,1)S(1)} %copy-done.8), kind=kOutput, calls=%fused_computation.48 | convolution fusion | flops 4297064448 | bytes 10485760 | tf_op jit(solution)/shard_map/dot_general | solution.py:105
  (52 shorter events, 8.8 us)
Async XLA Ops:
  0.0 1.6 copy-start
  8.5 3.3 copy-start.5
  8.5 4.4 %copy-start.6 = (bf16[1024,1024]{1,0:T(8,128)(2,1)S(1)}, bf16[1024,1024]{1,0:T(8,128)(2,1)}, u32[]{:S(2)}) copy-start(bf16[1024,1024]{1,0:T(8,128)(2,1)} %param.13) | copy-start | bytes 6291460
  17.6 3.1 copy-start.7
  42.7 281.3 %copy-start.3 = (s32[2048]{0:T(1024)S(1)}, s32[2048]{0:T(1024)}, u32[]{:S(2)}) copy-start(s32[2048]{0:T(1024)} %param.10) | copy-start | bytes 24580
  309.7 12.3 %collective-permute-start = (f32[8,128,128]{2,1,0:T(8,128)S(1)}, f32[8,128,128]{2,1,0:T(8,128)S(1)}, u32[]{:S(2)}, u32[]{:S(2)}) collective-permute-start(f32[8,128,128]{2,1,0:T(8,128)S(1)} %get-tuple-element.54), channel_id=1, source_target_pairs={{0,1},{1,2},{2,3},{3,4},{4,5},{5,6},{6,7},{7,8},{8,9},{9,10},{10,1... | collective-permute-start | bytes 1572872 | tf_op jit(solution)/shard_map/ppermute | solution.py:15
  322.0 20.8 %collective-permute-start.5 = (f32[8,128,128]{2,1,0:T(8,128)S(1)}, f32[8,128,128]{2,1,0:T(8,128)S(1)}, u32[]{:S(2)}, u32[]{:S(2)}) collective-permute-start(f32[8,128,128]{2,1,0:T(8,128)S(1)} %broadcast_select_fusion), channel_id=1, source_target_pairs={{0,1},{1,2},{2,3},{3,4},{4,5},{5,6},{6,7},{7,8},{8,9},{9,10},{10,1... | collective-permute-start | bytes 1572872 | tf_op jit(solution)/shard_map/ppermute | solution.py:15
  324.6 10.2 %collective-permute-start.3 = (s32[]{:T(128)}, s32[]{:T(128)}, u32[]{:S(2)}, u32[]{:S(2)}) collective-permute-start(s32[]{:T(128)} %bitcast.1), channel_id=1, source_target_pairs={{0,1},{1,2},{2,3},{3,4},{4,5},{5,6},{6,7},{7,8},{8,9},{9,10},{10,1... | collective-permute-start | bytes 20 | tf_op jit(solution)/shard_map/ppermute | solution.py:15
  326.5 12.5 %collective-permute-start.2 = (s32[]{:T(128)}, s32[]{:T(128)}, u32[]{:S(2)}, u32[]{:S(2)}) collective-permute-start(s32[]{:T(128)} %bitcast), channel_id=1, source_target_pairs={{0,1},{1,2},{2,3},{3,4},{4,5},{5,6},{6,7},{7,8},{8,9},{9,10},{10,1... | collective-permute-start | bytes 20 | tf_op jit(solution)/shard_map/ppermute | solution.py:15
  329.8 8.5 %collective-permute-start.1 = (s32[]{:T(128)}, s32[]{:T(128)}, u32[]{:S(2)}, u32[]{:S(2)}) collective-permute-start(s32[]{:T(128)} %convert_element_type.61), channel_id=1, source_target_pairs={{0,1},{1,2},{2,3},{3,4},{4,5},{5,6},{6,7},{7,8},{8,9},{9,10},{10,1... | collective-permute-start | bytes 20 | tf_op jit(solution)/shard_map/ppermute | solution.py:15
  335.4 6.8 %collective-permute-start.4 = (s32[]{:T(128)}, s32[]{:T(128)}, u32[]{:S(2)}, u32[]{:S(2)}) collective-permute-start(s32[]{:T(128)} %select_n.104), channel_id=1, source_target_pairs={{0,1},{1,2},{2,3},{3,4},{4,5},{5,6},{6,7},{7,8},{8,9},{9,10},{10,1... | collective-permute-start | bytes 20 | tf_op jit(solution)/shard_map/ppermute | solution.py:15
  342.9 25.1 %collective-permute-start.9 = (f32[8,128,128]{2,1,0:T(8,128)S(1)}, f32[8,128,128]{2,1,0:T(8,128)S(1)}, u32[]{:S(2)}, u32[]{:S(2)}) collective-permute-start(f32[8,128,128]{2,1,0:T(8,128)S(1)} %select_add_fusion.2), channel_id=1, source_target_pairs={{0,2},{1,3},{2,4},{3,5},{4,6},{5,7},{6,8},{7,9},{8,10},{9,11},{10,... | collective-permute-start | bytes 1572872 | tf_op jit(solution)/shard_map/ppermute | solution.py:15
  344.9 18.5 %collective-permute-start.6 = (s32[]{:T(128)}, s32[]{:T(128)}, u32[]{:S(2)}, u32[]{:S(2)}) collective-permute-start(s32[]{:T(128)} %select_n.102), channel_id=1, source_target_pairs={{0,1},{1,2},{2,3},{3,4},{4,5},{5,6},{6,7},{7,8},{8,9},{9,10},{10,1... | collective-permute-start | bytes 20 | tf_op jit(solution)/shard_map/ppermute | solution.py:15
  348.6 15.3 %collective-permute-start.7 = (s32[]{:T(128)}, s32[]{:T(128)}, u32[]{:S(2)}, u32[]{:S(2)}) collective-permute-start(s32[]{:T(128)} %select_n.103), channel_id=1, source_target_pairs={{0,1},{1,2},{2,3},{3,4},{4,5},{5,6},{6,7},{7,8},{8,9},{9,10},{10,1... | collective-permute-start | bytes 20 | tf_op jit(solution)/shard_map/ppermute | solution.py:15
  360.1 7.2 %collective-permute-start.8 = (s32[]{:T(128)}, s32[]{:T(128)}, u32[]{:S(2)}, u32[]{:S(2)}) collective-permute-start(s32[]{:T(128)} %select_n.112), channel_id=1, source_target_pairs={{0,2},{1,3},{2,4},{3,5},{4,6},{5,7},{6,8},{7,9},{8,10},{9,11},{10,... | collective-permute-start | bytes 20 | tf_op jit(solution)/shard_map/ppermute | solution.py:15
  368.1 30.7 %collective-permute-start.13 = (f32[8,128,128]{2,1,0:T(8,128)S(1)}, f32[8,128,128]{2,1,0:T(8,128)S(1)}, u32[]{:S(2)}, u32[]{:S(2)}) collective-permute-start(f32[8,128,128]{2,1,0:T(8,128)S(1)} %select_add_fusion.1), channel_id=1, source_target_pairs={{0,4},{1,5},{2,6},{3,7},{4,8},{5,9},{6,10},{7,11},{8,12},{9,13},{1... | collective-permute-start | bytes 1572872 | tf_op jit(solution)/shard_map/ppermute | solution.py:15
  380.9 14.0 %collective-permute-start.10 = (s32[]{:T(128)}, s32[]{:T(128)}, u32[]{:S(2)}, u32[]{:S(2)}) collective-permute-start(s32[]{:T(128)} %mul.65), channel_id=1, source_target_pairs={{0,2},{1,3},{2,4},{3,5},{4,6},{5,7},{6,8},{7,9},{8,10},{9,11},{10,... | collective-permute-start | bytes 20 | tf_op jit(solution)/shard_map/ppermute | solution.py:15
  385.9 9.8 %collective-permute-start.11 = (s32[]{:T(128)}, s32[]{:T(128)}, u32[]{:S(2)}, u32[]{:S(2)}) collective-permute-start(s32[]{:T(128)} %select_n.111), channel_id=1, source_target_pairs={{0,2},{1,3},{2,4},{3,5},{4,6},{5,7},{6,8},{7,9},{8,10},{9,11},{10,... | collective-permute-start | bytes 20 | tf_op jit(solution)/shard_map/ppermute | solution.py:15
  391.7 6.4 %collective-permute-start.12 = (s32[]{:T(128)}, s32[]{:T(128)}, u32[]{:S(2)}, u32[]{:S(2)}) collective-permute-start(s32[]{:T(128)} %select_n.121), channel_id=1, source_target_pairs={{0,4},{1,5},{2,6},{3,7},{4,8},{5,9},{6,10},{7,11},{8,12},{9,13},{1... | collective-permute-start | bytes 20 | tf_op jit(solution)/shard_map/ppermute | solution.py:15
  398.8 3.7 copy-start.2
  402.4 7.0 %copy-start.4 = (f32[1024]{0:T(1024)S(1)}, f32[1024]{0:T(1024)}, u32[]{:S(2)}) copy-start(f32[1024]{0:T(1024)} %param.15) | copy-start | bytes 12292
  409.4 4.4 %copy-start.8 = (bf16[1024,1024]{1,0:T(8,128)(2,1)S(1)}, bf16[1024,1024]{1,0:T(8,128)(2,1)}, u32[]{:S(2)}) copy-start(bf16[1024,1024]{1,0:T(8,128)(2,1)} %param.14) | copy-start | bytes 6291460
  413.9 6.2 %copy-start.1 = (bf16[1024,1024]{1,0:T(8,128)(2,1)S(1)}, bf16[1024,1024]{1,0:T(8,128)(2,1)}, u32[]{:S(2)}) copy-start(bf16[1024,1024]{1,0:T(8,128)(2,1)} %param.12) | copy-start | bytes 6291460
where the time goes:
time: 426 us; the launch traced here: 420 us
  local copies, waits for them, and re-layouts  230 us (54%)
  matrix products  94 us (22%)
  starting transfers between devices  51.9 us (12%)
  waiting for transfers between devices  17.5 us (4%)
  loops' own time  10.2 us (2%)
  other arithmetic  8.21 us (2%)
  between operations  8.2 us (2%)
    dynamic_update_slice x8, local copies, waits for them, and re-layouts, local_pass(): lax.scan(step, init, (q_blocks, k_blocks, v_blocks, id_blocks))  178 us
    ppermute x14, starting transfers between devices, from_behind(): return lax.ppermute(x, axis, pairs)  51.9 us
    dot_general x4, matrix products, step(): jnp.einsum('hst,thd->shd', scores, v_b, preferred_element_type=jnp.float32)  27.8 us
    dot_general x5, matrix products, state_product(): jnp.einsum(form, queries, high_part, preferred_element_type=jnp.float32)  19.3 us
    ppermute x14, waiting for transfers between devices, from_behind(): return lax.ppermute(x, axis, pairs)  17.5 us
    unnamed x21, local copies, waits for them, and re-layouts  16.2 us
    dot_general x5, matrix products, state_product(): jnp.einsum(form, queries, low_part, preferred_element_type=jnp.float32)  16.1 us
    dynamic_slice x12, local copies, waits for them, and re-layouts, local_pass(): lax.scan(step, init, (q_blocks, k_blocks, v_blocks, id_blocks))  12.9 us
  transfers between devices with their start and end apart: 14, of which 4 were waited for; matrix products, arithmetic and copies ran while one was open for 3% of the time, Pallas kernels for 0%

commit v1 on v0

v1 whole, which is shorter than its diff:
```python
import functools

import jax
import jax.numpy as jnp
from jax import lax
from jax.experimental import pallas as pl
from jax.experimental.pallas import tpu as pltpu
from jax.sharding import PartitionSpec as P

D = 1024
H = 8
HD = 128
MOST_LEN = 16384
TILE = 512
CH = 256
MSG = HD + 8
MESH = pl.DeviceIdType.MESH
F32 = jnp.float32
BF16 = jnp.bfloat16


def dot(a, b):
    return jnp.dot(a, b, preferred_element_type=F32)


def kernel(
    n_outer, n_inner, group,
    ids, gain, hid_hbm, wq_hbm, wk_hbm, wv_hbm, wo_hbm, out_hbm,
    hid, wq, wk, wv, wo, qs, ks, vs, loc, outv, idc, st, sb, cb,
    msg1, got1, tail, prev, msg3, got3,
    hid_sem, w_sem, out_sem, s1, r1, s2, r2, s3, r3,
):
    tokens = hid.shape[0]
    tiles = tokens // TILE
    per = TILE // CH
    total = n_outer * n_inner
    groups = total // group
    me = lax.axis_index("outer") * n_inner + lax.axis_index("inner")
    g = me // group
    m = me % group

    def at(index):
        return (index // n_inner, index % n_inner)

    def peer(d):
        return (m + d) % group

    def hid_copy(i):
        rows = pl.ds(pl.multiple_of(i * TILE, TILE), TILE)
        return pltpu.make_async_copy(hid_hbm.at[rows], hid.at[rows], hid_sem.at[i])

    w_copies = [
        pltpu.make_async_copy(src, dst, w_sem.at[i])
        for i, (src, dst) in enumerate(((wk_hbm, wk), (wv_hbm, wv), (wq_hbm, wq), (wo_hbm, wo)))
    ]
    w_copies[0].start()
    hid_copy(0).start()
    w_copies[1].start()
    for i in range(1, tiles):
        hid_copy(i).start()
    w_copies[2].start()
    w_copies[3].start()

    barrier = pltpu.get_barrier_semaphore()
    for d in range(1, group):
        pl.semaphore_signal(barrier, inc=1, device_id=at(g * group + peer(d)), device_id_type=MESH)

    @pl.when(g > 0)
    def _():
        pl.semaphore_signal(barrier, inc=1, device_id=at(me - group), device_id_type=MESH)

    @pl.when(g < groups - 1)
    def _():
        pl.semaphore_signal(barrier, inc=1, device_id=at(me + group), device_id_type=MESH)

    for r in range(tokens // 128):
        row = ids[r : r + 1, :].astype(F32)
        idc[r * 128 : (r + 1) * 128, :] = jnp.transpose(jnp.broadcast_to(row, (128, 128)))
    st[...] = jnp.zeros_like(st)

    def last_of(c):
        return idc[pl.ds(pl.multiple_of(c * CH + CH - 8, 8), 8), :][7:8, :]

    def before(c):
        return idc[pl.ds(pl.multiple_of(jnp.maximum(c * CH - 8, 0), 8), 8), :][7:8, :]

    w_copies[0].wait()
    w_copies[1].wait()

    def project(i, carry):
        hid_copy(i).wait()
        rows = pl.ds(pl.multiple_of(i * TILE, TILE), TILE)
        x = hid[rows, :]
        ks[rows, :] = dot(x, wk[...]).astype(BF16)
        vs[rows, :] = dot(x, wv[...]).astype(BF16)
        for j in range(per):
            c = i * per + j
            part = pl.ds(pl.multiple_of(c * CH, CH), CH)
            last = last_of(c)
            held = last == before(c)
            mask = jnp.where(idc[part, :] == last, 1.0, 0.0).astype(BF16)
            for h in range(H):
                lanes = slice(h * HD, (h + 1) * HD)
                state = st[h]
                sb[c, h] = state.astype(BF16)
                add = lax.dot_general(
                    ks[part, lanes] * mask, vs[part, lanes], (((0,), (0,)), ((), ())),
                    preferred_element_type=F32,
                )
                st[h] = jnp.where(held, state, 0.0) + add
        return carry

    lax.fori_loop(0, tiles, project, 0)

    my_last = jnp.broadcast_to(last_of(tokens // CH - 1), (8, 128))
    for h in range(H):
        msg1[h, 0:HD, :] = st[h]
        msg1[h, HD:MSG, :] = my_last
    got1[pl.ds(m, 1)] = msg1[pl.ds(m, 1)]

    @pl.when(g == 0)
    def _():
        prev[0:HD, :] = jnp.zeros((HD, HD), F32)
        prev[HD:MSG, :] = jnp.full((8, HD), -1.0, F32)

    has_prev = jnp.where(g > 0, 1, 0)
    has_next = jnp.where(g < groups - 1, 1, 0)
    pl.semaphore_wait(barrier, group - 1 + has_prev + has_next)

    def copy1(d):
        return pltpu.make_async_remote_copy(
            src_ref=msg1.at[peer(d)], dst_ref=got1.at[m],
            send_sem=s1.at[d - 1], recv_sem=r1.at[d - 1],
            device_id=at(g * group + peer(d)), device_id_type=MESH,
        )

    def copy2():
        return pltpu.make_async_remote_copy(
            src_ref=tail, dst_ref=prev, send_sem=s2, recv_sem=r2,
            device_id=at(me + group), device_id_type=MESH,
        )

    def copy3(d):
        return pltpu.make_async_remote_copy(
            src_ref=msg3.at[peer(d)], dst_ref=got3.at[m],
            send_sem=s3.at[d - 1], recv_sem=r3.at[d - 1],
            device_id=at(g * group + peer(d)), device_id_type=MESH,
        )

    for d in range(1, group):
        copy1(d).start()

    def exchange_tail():
        for d in range(1, group):
            copy1(d).wait_recv()
        state = got1[0, 0:HD, :]
        for j in range(1, group):
            same = got1[j, HD : HD + 1, :] == got1[j - 1, HD : HD + 1, :]
            state = got1[j, 0:HD, :] + jnp.where(same, state, 0.0)
        tail[0:HD, :] = state
        tail[HD:MSG, :] = got1[group - 1, HD:MSG, :]

        @pl.when(g < groups - 1)
        def _():
            copy2().start()

    def exchange_prefix():
        @pl.when(g > 0)
        def _():
            copy2().wait_recv()

        msg3[0] = prev[...]
        for j in range(group - 1):
            before_id = msg3[j, HD : HD + 1, :]
            same = got1[j, HD : HD + 1, :] == before_id
            msg3[j + 1, 0:HD, :] = got1[j, 0:HD, :] + jnp.where(same, msg3[j, 0:HD, :], 0.0)
            msg3[j + 1, HD:MSG, :] = got1[j, HD:MSG, :]
        got3[pl.ds(m, 1)] = msg3[pl.ds(m, 1)]
        for d in range(1, group):
            copy3(d).start()

    w_copies[2].wait()
    s_of = lax.broadcasted_iota(jnp.int32, (CH, CH), 0)
    t_of = lax.broadcasted_iota(jnp.int32, (CH, CH), 1)

    def attend(i, carry):
        @pl.when(i == tiles // 2)
        def _():
            exchange_tail()

        @pl.when(i == tiles - 1)
        def _():
            exchange_prefix()

        rows = pl.ds(pl.multiple_of(i * TILE, TILE), TILE)
        qs[rows, :] = dot(hid[rows, :], wq[...]).astype(BF16)
        for j in range(per):
            c = i * per + j
            part = pl.ds(pl.multiple_of(c * CH, CH), CH)
            col = idc[part, :]
            row = jnp.concatenate(
                [ids[pl.ds(c * (CH // 128) + r, 1), :].astype(F32) for r in range(CH // 128)], axis=1
            )
            keep = (jnp.concatenate([col] * (CH // 128), axis=1) == row) & (t_of <= s_of)
            mask = jnp.where(keep, 1.0, 0.0).astype(BF16)
            old = jnp.where(col == before(c), 1.0, 0.0).astype(BF16)
            for h in range(H):
                lanes = slice(h * HD, (h + 1) * HD)
                q = qs[part, lanes]
                scores = lax.dot_general(
                    q, ks[part, lanes], (((1,), (1,)), ((), ())), preferred_element_type=F32
                )
                scores = scores.astype(BF16) * mask
                loc[part, lanes] = dot(scores, vs[part, lanes]) + dot(q * old, sb[c, h])
        return carry

    lax.fori_loop(0, tiles, attend, 0)

    for d in range(1, group):
        copy3(d).wait_recv()
    for h in range(H):
        cb[h] = got3[h, 0:HD, :].astype(BF16)
    carry_id = got3[0, HD : HD + 1, :]
    w_copies[3].wait()

    def out_copy(i):
        rows = pl.ds(pl.multiple_of(i * TILE, TILE), TILE)
        return pltpu.make_async_copy(outv.at[rows], out_hbm.at[rows], out_sem.at[i])

    def finish(i, carry):
        rows = pl.ds(pl.multiple_of(i * TILE, TILE), TILE)
        old = jnp.where(idc[rows, :] == carry_id, 1.0, 0.0).astype(BF16)
        normed = []
        for h in range(H):
            lanes = slice(h * HD, (h + 1) * HD)
            mixed = loc[rows, lanes] + dot(qs[rows, lanes] * old, cb[h])
            scale = lax.rsqrt(jnp.mean(mixed * mixed, axis=1, keepdims=True) + 1e-6)
            normed.append((mixed * scale * gain[:, lanes]).astype(BF16))
        outv[rows, :] = dot(jnp.concatenate(normed, axis=1), wo[...]).astype(BF16)
        out_copy(i).start()
        return carry

    lax.fori_loop(0, tiles, finish, 0)

    for i in range(tiles):
        out_copy(i).wait()
    for d in range(1, group):
        copy1(d).wait_send()
        copy3(d).wait_send()

    @pl.when(g < groups - 1)
    def _():
        copy2().wait_send()


def body(n_outer, n_inner, hidden, segment_ids, wq, wk, wv, wo, gain):
    tokens = hidden.shape[0]
    group = MOST_LEN // tokens
    chunks = tokens // CH
    vm = pl.BlockSpec(memory_space=pltpu.VMEM)
    hbm = pl.BlockSpec(memory_space=pl.ANY)
    dma = pltpu.SemaphoreType.DMA
    weight = pltpu.VMEM((D, D), BF16)
    wide = pltpu.VMEM((tokens, D), BF16)
    msgs = pltpu.VMEM((group, MSG, HD), F32)
    one = pltpu.VMEM((MSG, HD), F32)
    call = pl.pallas_call(
        functools.partial(kernel, n_outer, n_inner, group),
        out_shape=jax.ShapeDtypeStruct((tokens, D), BF16),
        in_specs=[vm, vm, hbm, hbm, hbm, hbm, hbm],
        out_specs=hbm,
        scratch_shapes=[
            wide, weight, weight, weight, weight, wide, wide, wide,
            pltpu.VMEM((tokens, D), F32), wide,
            pltpu.VMEM((tokens, 128), F32),
            pltpu.VMEM((H, HD, HD), F32),
            pltpu.VMEM((chunks, H, HD, HD), BF16),
            pltpu.VMEM((H, HD, HD), BF16),
            msgs, msgs, one, one, msgs, msgs,
            dma((tokens // TILE,)), dma((4,)), dma((tokens // TILE,)),
            dma((group - 1,)), dma((group - 1,)), dma, dma, dma((group - 1,)), dma((group - 1,)),
        ],
        compiler_params=pltpu.CompilerParams(
            collective_id=0, has_side_effects=True, vmem_limit_bytes=58 * 1024 * 1024
        ),
        cost_estimate=pl.CostEstimate(flops=22 * 10**9, bytes_accessed=16 * 2**20, transcendentals=0),
    )
    return call(
        segment_ids.reshape(tokens // 128, 128), gain.reshape(1, D), hidden, wq, wk, wv, wo
    )


def solution(mesh):
    both = ("outer", "inner")
    in_specs = (P(both, None), P(both), P(), P(), P(), P(), P())
    run = functools.partial(body, mesh.shape["outer"], mesh.shape["inner"])
    return jax.shard_map(run, mesh=mesh, in_specs=in_specs, out_specs=P(both, None), check_vma=False)
```

time: 426 us -> 47.3 us (0.11)
  the two profiles are of different devices: /device:TPU:8 before, /device:TPU:1 now
where the time goes in v1:
time: 47.3 us; the launch traced here: 47 us
  Pallas kernels  42.4 us (90%)
  local copies, waits for them, and re-layouts  4.64 us (10%)
    pallas_call x1, Pallas kernels, body(): call(segment_ids.reshape(tokens // 128, 128), gain.reshape(1, D), hidden,...  42.4 us
    unnamed x1, local copies, waits for them, and re-layouts  4.64 us

profile of v1, /device:TPU:1, one launch (start us, length us, event | category | flops | bytes accessed | tf_op | source)
XLA Modules:
  0.0 47.0 jit_solution(3441357431958945797)
XLA Ops:
  0.0 42.4 %shard_map.73 = bf16[2048,1024]{1,0:T(8,128)(2,1)} custom-call(s32[16,128]{1,0:T(8,128)} %bitcast.2, f32[1,1024]{1,0:T(1,128)} %bitcast.3, bf16[2048,1024]{1,0:T(8,128)(2,1)} %hid_hbm.1, bf16[1024,1024]{1,0:T(8,128)(2,1)} %wq_hbm.1, bf16[1024,1024]{1,0:T(8,128)(2,1)} %wk_hbm.1, bf16[1024,1024]{1,0:T(8,128)(2,1)} %wv_hbm.1, bf16[1024,1024]{1,0:T(8,128)(2,1)} %wo_hbm.1), custom_call_target="tpu_custom_call" | custom-call | flops 22000001024 | bytes 16777216 | tf_op jit(solution)/shard_map/pallas_call | solution.py:288
  42.4 4.6 %copy.9 = bf16[2048,1024]{1,0:T(8,128)(2,1)} copy(bf16[2048,1024]{1,0:T(8,128)(2,1)} %shard_map.73) | data formatting | bytes 8388608

commit v2 on v1

v2 whole, which is shorter than its diff:
```python
import functools

import jax
import jax.numpy as jnp
from jax import lax
from jax.experimental import pallas as pl
from jax.experimental.pallas import tpu as pltpu
from jax.sharding import PartitionSpec as P

D = 1024
H = 8
HD = 128
MOST_LEN = 16384
TILE = 512
CH = 256
LAST = 256
MSG = HD + 8
MESH = pl.DeviceIdType.MESH
F32 = jnp.float32
BF16 = jnp.bfloat16


def dot(a, b):
    return jnp.dot(a, b, preferred_element_type=F32)


def column(ids_row):
    return jnp.transpose(jnp.broadcast_to(ids_row.astype(F32), (128, 128)))


def kernel(
    n_outer, n_inner, group,
    ids, hid_hbm, wq_hbm, wk_hbm, wv_hbm, q_hbm, loc_hbm, carry, carry_id,
    hid, wq, wk, wv, qs, ks, vs, loc, idc, sb,
    msg1, got1, tail, prev, msg3, got3,
    hid_sem, w_sem, q_sem, loc_sem, s1, r1, s2, r2, s3, r3,
):
    tokens = hid.shape[0]
    tiles = tokens // TILE
    per = TILE // CH
    total = n_outer * n_inner
    groups = total // group
    half = H // 2
    me = lax.axis_index("outer") * n_inner + lax.axis_index("inner")
    g = me // group
    m = me % group
    parity = m % 2
    mine = parity * half + m // 2

    def at(index):
        return (index // n_inner, index % n_inner)

    def peer(d):
        return (m + d) % group

    def rows_of(i):
        return pl.ds(pl.multiple_of(i * TILE, TILE), TILE)

    def hid_copy(i):
        return pltpu.make_async_copy(hid_hbm.at[rows_of(i)], hid.at[rows_of(i)], hid_sem.at[i])

    def half_copies(p):
        cols = slice(p * half * HD, (p + 1) * half * HD)
        return (
            pltpu.make_async_copy(wk_hbm.at[:, cols], wk.at[:, cols], w_sem.at[2 * p]),
            pltpu.make_async_copy(wv_hbm.at[:, cols], wv.at[:, cols], w_sem.at[2 * p + 1]),
        )

    wq_copy = pltpu.make_async_copy(wq_hbm, wq, w_sem.at[4])
    first = half_copies(0)
    first[0].start()
    hid_copy(0).start()
    first[1].start()
    for i in range(1, tiles):
        hid_copy(i).start()
    for copy in half_copies(1):
        copy.start()
    wq_copy.start()

    barrier = pltpu.get_barrier_semaphore()
    for d in range(1, group):
        pl.semaphore_signal(barrier, inc=1, device_id=at(g * group + peer(d)), device_id_type=MESH)

    @pl.when(g > 0)
    def _():
        pl.semaphore_signal(barrier, inc=1, device_id=at(me - group), device_id_type=MESH)

    @pl.when(g < groups - 1)
    def _():
        pl.semaphore_signal(barrier, inc=1, device_id=at(me + group), device_id_type=MESH)

    for r in range(tokens // 128):
        idc[r * 128 : (r + 1) * 128, :] = column(ids[r : r + 1, :])

    def last_of(c):
        return idc[pl.ds(pl.multiple_of(c * CH + CH - 8, 8), 8), :][7:8, :]

    def before(c):
        return idc[pl.ds(pl.multiple_of(jnp.maximum(c * CH - 8, 0), 8), 8), :][7:8, :]

    my_last = jnp.broadcast_to(last_of(tokens // CH - 1), (8, 128))
    for h in range(H):
        msg1[h, 0:HD, :] = jnp.zeros((HD, HD), F32)
        msg1[h, HD:MSG, :] = my_last

    @pl.when(g == 0)
    def _():
        prev[0:HD, :] = jnp.zeros((HD, HD), F32)
        prev[HD:MSG, :] = jnp.full((8, HD), -1.0, F32)

    def copy1(d):
        to = peer(d)
        return pltpu.make_async_remote_copy(
            src_ref=msg1.at[(to % 2) * half + to // 2], dst_ref=got1.at[m],
            send_sem=s1.at[d], recv_sem=r1.at[d],
            device_id=at(g * group + to), device_id_type=MESH,
        )

    def copy2():
        return pltpu.make_async_remote_copy(
            src_ref=tail, dst_ref=prev, send_sem=s2, recv_sem=r2,
            device_id=at(me + group), device_id_type=MESH,
        )

    def copy3(d):
        return pltpu.make_async_remote_copy(
            src_ref=msg3.at[peer(d)], dst_ref=got3.at[mine],
            send_sem=s3.at[d], recv_sem=r3.at[d],
            device_id=at(g * group + peer(d)), device_id_type=MESH,
        )

    def send_half(p):
        odd = (parity + p) % 2
        for k in range(group // 2):
            if k > 0:
                copy1(2 * k + odd).start()
            else:
                @pl.when(odd == 1)
                def _():
                    copy1(1).start()

                @pl.when(odd == 0)
                def _():
                    got1[pl.ds(m, 1)] = msg1[pl.ds(mine, 1)]

    def exchange_tail():
        for d in range(1, group):
            copy1(d).wait_recv()
        state = got1[0, 0:HD, :]
        for j in range(1, group):
            same = got1[j, HD : HD + 1, :] == got1[j - 1, HD : HD + 1, :]
            state = got1[j, 0:HD, :] + jnp.where(same, state, 0.0)
        tail[0:HD, :] = state
        tail[HD:MSG, :] = got1[group - 1, HD:MSG, :]

        @pl.when(g < groups - 1)
        def _():
            copy2().start()

    def exchange_prefix():
        @pl.when(g > 0)
        def _():
            copy2().wait_recv()

        msg3[0] = prev[...]
        for j in range(group - 1):
            before_id = msg3[j, HD : HD + 1, :]
            same = got1[j, HD : HD + 1, :] == before_id
            msg3[j + 1, 0:HD, :] = got1[j, 0:HD, :] + jnp.where(same, msg3[j, 0:HD, :], 0.0)
            msg3[j + 1, HD:MSG, :] = got1[j, HD:MSG, :]
        got3[pl.ds(mine, 1)] = msg3[pl.ds(m, 1)]
        for d in range(1, group):
            copy3(d).start()

    def project(p):
        cols = slice(p * half * HD, (p + 1) * half * HD)

        def tile(i, unused):
            if p == 0:
                hid_copy(i).wait()
            rows = rows_of(i)
            x = hid[rows, :]
            ks[rows, cols] = dot(x, wk[:, cols]).astype(BF16)
            vs[rows, cols] = dot(x, wv[:, cols]).astype(BF16)
            for j in range(per):
                c = i * per + j
                part = pl.ds(pl.multiple_of(c * CH, CH), CH)
                last = last_of(c)
                held = last == before(c)
                mask = jnp.where(idc[part, :] == last, 1.0, 0.0).astype(BF16)
                for h in range(p * half, (p + 1) * half):
                    lanes = slice(h * HD, (h + 1) * HD)
                    state = msg1[h, 0:HD, :]
                    sb[c, h] = state.astype(BF16)
                    add = lax.dot_general(
                        ks[part, lanes] * mask, vs[part, lanes], (((0,), (0,)), ((), ())),
                        preferred_element_type=F32,
                    )
                    msg1[h, 0:HD, :] = jnp.where(held, state, 0.0) + add
            return unused

        for copy in half_copies(p):
            copy.wait()
        lax.fori_loop(0, tiles, tile, 0)

    project(0)
    has_prev = jnp.where(g > 0, 1, 0)
    has_next = jnp.where(g < groups - 1, 1, 0)
    pl.semaphore_wait(barrier, group - 1 + has_prev + has_next)
    send_half(0)
    project(1)
    send_half(1)

    @pl.when(parity == 0)
    def _():
        exchange_tail()

    wq_copy.wait()
    s_of = lax.broadcasted_iota(jnp.int32, (CH, CH), 0)
    t_of = lax.broadcasted_iota(jnp.int32, (CH, CH), 1)

    def q_copy(i):
        return pltpu.make_async_copy(qs.at[rows_of(i)], q_hbm.at[rows_of(i)], q_sem.at[i])

    def loc_copy(i):
        return pltpu.make_async_copy(loc.at[rows_of(i)], loc_hbm.at[rows_of(i)], loc_sem.at[i])

    def attend(i, unused):
        @pl.when((i == 1) & (parity == 0))
        def _():
            exchange_prefix()

        rows = rows_of(i)
        qs[rows, :] = dot(hid[rows, :], wq[...]).astype(BF16)

        @pl.when((i == 1) & (parity == 1))
        def _():
            exchange_tail()

        @pl.when((i == 2) & (parity == 1))
        def _():
            exchange_prefix()

        for j in range(per):
            c = i * per + j
            part = pl.ds(pl.multiple_of(c * CH, CH), CH)
            col = idc[part, :]
            row = jnp.concatenate(
                [ids[pl.ds(c * (CH // 128) + r, 1), :].astype(F32) for r in range(CH // 128)], axis=1
            )
            keep = (jnp.concatenate([col] * (CH // 128), axis=1) == row) & (t_of <= s_of)
            mask = jnp.where(keep, 1.0, 0.0).astype(BF16)
            old = jnp.where(col == before(c), 1.0, 0.0).astype(BF16)
            for h in range(H):
                lanes = slice(h * HD, (h + 1) * HD)
                q = qs[part, lanes]
                scores = lax.dot_general(
                    q, ks[part, lanes], (((1,), (1,)), ((), ())), preferred_element_type=F32
                )
                scores = scores.astype(BF16) * mask
                mixed = dot(scores, vs[part, lanes]) + dot(q * old, sb[c, h])
                loc[part, lanes] = mixed.astype(BF16)
        q_copy(i).start()
        loc_copy(i).start()
        return unused

    lax.fori_loop(0, tiles, attend, 0)

    for d in range(1, group):
        copy3(d).wait_recv()
    for h in range(H):
        carry[h] = got3[h, 0:HD, :].astype(BF16)
    carry_id[...] = got3[0, HD:MSG, :]

    for d in range(1, group):
        copy1(d).wait_send()
        copy3(d).wait_send()

    @pl.when(g < groups - 1)
    def _():
        copy2().wait_send()

    for i in range(tiles):
        q_copy(i).wait()
        loc_copy(i).wait()


def finish(ids, carry_id, gain, carry, q_ref, loc_ref, wo, out):
    tile = q_ref.shape[0]
    steps = tile // 128
    first = pl.program_id(0) * steps
    col = jnp.concatenate([column(ids[pl.ds(first + r, 1), :]) for r in range(steps)], axis=0)
    old = jnp.where(col == carry_id[0:1, :], 1.0, 0.0).astype(BF16)
    normed = []
    for h in range(H):
        lanes = slice(h * HD, (h + 1) * HD)
        mixed = loc_ref[:, lanes].astype(F32) + dot(q_ref[:, lanes] * old, carry[h])
        scale = lax.rsqrt(jnp.mean(mixed * mixed, axis=1, keepdims=True) + 1e-6)
        normed.append((mixed * scale * gain[:, lanes]).astype(BF16))
    out[...] = dot(jnp.concatenate(normed, axis=1), wo[...]).astype(BF16)


def body(n_outer, n_inner, hidden, segment_ids, wq, wk, wv, wo, gain):
    tokens = hidden.shape[0]
    group = MOST_LEN // tokens
    chunks = tokens // CH
    vm = pl.BlockSpec(memory_space=pltpu.VMEM)
    hbm = pl.BlockSpec(memory_space=pl.ANY)
    dma = pltpu.SemaphoreType.DMA
    weight = pltpu.VMEM((D, D), BF16)
    wide = pltpu.VMEM((tokens, D), BF16)
    msgs = pltpu.VMEM((group, MSG, HD), F32)
    one = pltpu.VMEM((MSG, HD), F32)
    ids = segment_ids.reshape(tokens // 128, 128)
    tiles = tokens // TILE
    local = pl.pallas_call(
        functools.partial(kernel, n_outer, n_inner, group),
        out_shape=[
            jax.ShapeDtypeStruct((tokens, D), BF16),
            jax.ShapeDtypeStruct((tokens, D), BF16),
            jax.ShapeDtypeStruct((H, HD, HD), BF16),
            jax.ShapeDtypeStruct((8, HD), F32),
        ],
        in_specs=[vm, hbm, hbm, hbm, hbm],
        out_specs=[hbm, hbm, vm, vm],
        scratch_shapes=[
            wide, weight, weight, weight, wide, wide, wide, wide,
            pltpu.VMEM((tokens, 128), F32),
            pltpu.VMEM((chunks, H, HD, HD), BF16),
            msgs, msgs, one, one, msgs, msgs,
            dma((tiles,)), dma((5,)), dma((tiles,)), dma((tiles,)),
            dma((group,)), dma((group,)), dma, dma, dma((group,)), dma((group,)),
        ],
        compiler_params=pltpu.CompilerParams(
            collective_id=0, has_side_effects=True, vmem_limit_bytes=54 * 2**20
        ),
        cost_estimate=pl.CostEstimate(flops=17 * 10**9, bytes_accessed=18 * 2**20, transcendentals=0),
    )
    queries, mixed, carry, carry_id = local(ids, hidden, wq, wk, wv)

    def whole(shape):
        return pl.BlockSpec(shape, lambda i: (0,) * len(shape))

    step = pl.BlockSpec((LAST, D), lambda i: (i, 0))
    return pl.pallas_call(
        finish,
        grid=(tokens // LAST,),
        out_shape=jax.ShapeDtypeStruct((tokens, D), BF16),
        in_specs=[
            whole(ids.shape), whole((8, HD)), whole((1, D)), whole((H, HD, HD)), step, step, whole((D, D)),
        ],
        out_specs=step,
        compiler_params=pltpu.CompilerParams(vmem_limit_bytes=58 * 2**20),
        cost_estimate=pl.CostEstimate(flops=5 * 10**9, bytes_accessed=14 * 2**20, transcendentals=0),
    )(ids, carry_id, gain.reshape(1, D), carry, queries, mixed, wo)


def solution(mesh):
    both = ("outer", "inner")
    in_specs = (P(both, None), P(both), P(), P(), P(), P(), P())
    run = functools.partial(body, mesh.shape["outer"], mesh.shape["inner"])
    return jax.shard_map(run, mesh=mesh, in_specs=in_specs, out_specs=P(both, None), check_vma=False)
```

time: 47.3 us -> 45.2 us (0.956)
  local copies, waits for them, and re-layouts: 4.64 us -> 0 us
  Pallas kernels: 42.4 us -> 44.8 us
    unnamed x1 -> x0, local copies, waits for them, and re-layouts: 4.64 us -> none
    pallas_call x1 -> x2, Pallas kernels: 42.4 us -> 44.8 us  [the longest x1 32.3 us: body(): queries, mixed, carry, carry_id = local(ids, hidden, wq, wk, wv)]
where the time goes in v2:
time: 45.2 us; the launch traced here: 44.9 us
  Pallas kernels  44.8 us (99%)
    pallas_call x1, Pallas kernels, body(): queries, mixed, carry, carry_id = local(ids, hidden, wq, wk, wv)  32.3 us
    pallas_call x1, Pallas kernels, body(): pl.pallas_call(finish, grid=(tokens // LAST,), out_shape=jax.ShapeDtypeSt...  12.5 us

profile of v2, /device:TPU:1, one launch (start us, length us, event | category | flops | bytes accessed | tf_op | source)
XLA Modules:
  0.0 44.9 jit_solution(3986075837527835083)
XLA Ops:
  0.0 32.3 %shard_map.73 = (bf16[2048,1024]{1,0:T(8,128)(2,1)}, bf16[2048,1024]{1,0:T(8,128)(2,1)}, bf16[8,128,128]{2,1,0:T(8,128)(2,1)}, f32[8,128]{1,0:T(8,128)}) custom-call(s32[16,128]{1,0:T(8,128)} %bitcast.2, bf16[2048,1024]{1,0:T(8,128)(2,1)} %hid_hbm.1, bf16[1024,1024]{1,0:T(8,128)(2,1)} %wq_hbm.1, bf16[1024,1024]{1,0:T(8,128)(2,1)} %wk_hbm.1, ...), custom_call_target="tpu_custom_call" | custom-call | flops 16999999488 | bytes 18874368 | tf_op jit(solution)/shard_map/pallas_call | solution.py:339
  32.3 12.5 %shard_map.74 = bf16[2048,1024]{1,0:T(8,128)(2,1)} custom-call(s32[16,128]{1,0:T(8,128)} %bitcast.3, f32[8,128]{1,0:T(8,128)} %get-tuple-element.9.carry_id, f32[1,1024]{1,0:T(1,128)} %bitcast.4, bf16[8,128,128]{2,1,0:T(8,128)(2,1)} %get-tuple-element.10.carry, bf16[2048,1024]{1,0:T(8,128)(2,1)} %get-tuple-element.11.q_ref, ...), custom_call_target="tpu_custom_call" | custom-call | flops 5000000000 | bytes 14680064 | tf_op jit(solution)/shard_map/pallas_call | solution.py:345

commit v3 on v2

--- a/solution.py
+++ b/solution.py
@@ -13,7 +13,7 @@
 MOST_LEN = 16384
 TILE = 512
 CH = 256
-LAST = 256
+LAST = 512
 MSG = HD + 8
 MESH = pl.DeviceIdType.MESH
 F32 = jnp.float32
@@ -291,11 +291,18 @@
     first = pl.program_id(0) * steps
     col = jnp.concatenate([column(ids[pl.ds(first + r, 1), :]) for r in range(steps)], axis=0)
     old = jnp.where(col == carry_id[0:1, :], 1.0, 0.0).astype(BF16)
+    pair = 2 * HD
+    r_head = lax.broadcasted_iota(jnp.int32, (pair, pair), 0) // HD
+    c_head = lax.broadcasted_iota(jnp.int32, (pair, pair), 1) // HD
+    average = jnp.where(r_head == c_head, 1.0 / HD, 0.0).astype(BF16)
     normed = []
-    for h in range(H):
-        lanes = slice(h * HD, (h + 1) * HD)
-        mixed = loc_ref[:, lanes].astype(F32) + dot(q_ref[:, lanes] * old, carry[h])
-        scale = lax.rsqrt(jnp.mean(mixed * mixed, axis=1, keepdims=True) + 1e-6)
+    for p in range(H // 2):
+        lanes = slice(p * pair, (p + 1) * pair)
+        carried = [
+            dot(q_ref[:, h * HD : (h + 1) * HD] * old, carry[h]) for h in (2 * p, 2 * p + 1)
+        ]
+        mixed = loc_ref[:, lanes].astype(F32) + jnp.concatenate(carried, axis=1)
+        scale = lax.rsqrt(dot((mixed * mixed).astype(BF16), average) + 1e-6)
         normed.append((mixed * scale * gain[:, lanes]).astype(BF16))
     out[...] = dot(jnp.concatenate(normed, axis=1), wo[...]).astype(BF16)
 

time: 45.2 us -> 44.6 us (0.987)
  Pallas kernels: 44.8 us -> 44.3 us
    pallas_call x1, Pallas kernels: 12.5 us -> 12 us  [body(): pl.pallas_call(finish, grid=(tokens // LAST,), out_shape=jax.ShapeDtypeSt...]
where the time goes in v3:
time: 44.6 us; the launch traced here: 44.4 us
  Pallas kernels  44.3 us (99%)
    pallas_call x1, Pallas kernels, body(): queries, mixed, carry, carry_id = local(ids, hidden, wq, wk, wv)  32.3 us
    pallas_call x1, Pallas kernels, body(): pl.pallas_call(finish, grid=(tokens // LAST,), out_shape=jax.ShapeDtypeSt...  12 us

profile of v3, /device:TPU:1, one launch (start us, length us, event | category | flops | bytes accessed | tf_op | source)
XLA Modules:
  0.0 44.4 jit_solution(13364960501870683240)
XLA Ops:
  0.0 32.3 %shard_map.73 = (bf16[2048,1024]{1,0:T(8,128)(2,1)}, bf16[2048,1024]{1,0:T(8,128)(2,1)}, bf16[8,128,128]{2,1,0:T(8,128)(2,1)}, f32[8,128]{1,0:T(8,128)}) custom-call(s32[16,128]{1,0:T(8,128)} %bitcast.2, bf16[2048,1024]{1,0:T(8,128)(2,1)} %hid_hbm.1, bf16[1024,1024]{1,0:T(8,128)(2,1)} %wq_hbm.1, bf16[1024,1024]{1,0:T(8,128)(2,1)} %wk_hbm.1, ...), custom_call_target="tpu_custom_call" | custom-call | flops 16999999488 | bytes 18874368 | tf_op jit(solution)/shard_map/pallas_call | solution.py:346
  32.3 12.0 %shard_map.74 = bf16[2048,1024]{1,0:T(8,128)(2,1)} custom-call(s32[16,128]{1,0:T(8,128)} %bitcast.3, f32[8,128]{1,0:T(8,128)} %get-tuple-element.9.carry_id, f32[1,1024]{1,0:T(1,128)} %bitcast.4, bf16[8,128,128]{2,1,0:T(8,128)(2,1)} %get-tuple-element.10.carry, bf16[2048,1024]{1,0:T(8,128)(2,1)} %get-tuple-element.11.q_ref, ...), custom_call_target="tpu_custom_call" | custom-call | flops 5000000000 | bytes 14680064 | tf_op jit(solution)/shard_map/pallas_call | solution.py:352

commit v4 on v3

--- a/solution.py
+++ b/solution.py
@@ -12,7 +12,7 @@
 HD = 128
 MOST_LEN = 16384
 TILE = 512
-CH = 256
+CH = 128
 LAST = 512
 MSG = HD + 8
 MESH = pl.DeviceIdType.MESH

time: 44.6 us -> 43.1 us (0.966)
  Pallas kernels: 44.3 us -> 42.9 us
    pallas_call x1, Pallas kernels: 32.3 us -> 30.9 us  [body(): queries, mixed, carry, carry_id = local(ids, hidden, wq, wk, wv)]
where the time goes in v4:
time: 43.1 us; the launch traced here: 42.9 us
  Pallas kernels  42.9 us (100%)
    pallas_call x1, Pallas kernels, body(): queries, mixed, carry, carry_id = local(ids, hidden, wq, wk, wv)  30.9 us
    pallas_call x1, Pallas kernels, body(): pl.pallas_call(finish, grid=(tokens // LAST,), out_shape=jax.ShapeDtypeSt...  12 us

profile of v4, /device:TPU:1, one launch (start us, length us, event | category | flops | bytes accessed | tf_op | source)
XLA Modules:
  0.0 42.9 jit_solution(2521455823315730690)
XLA Ops:
  0.0 30.9 %shard_map.73 = (bf16[2048,1024]{1,0:T(8,128)(2,1)}, bf16[2048,1024]{1,0:T(8,128)(2,1)}, bf16[8,128,128]{2,1,0:T(8,128)(2,1)}, f32[8,128]{1,0:T(8,128)}) custom-call(s32[16,128]{1,0:T(8,128)} %bitcast.2, bf16[2048,1024]{1,0:T(8,128)(2,1)} %hid_hbm.1, bf16[1024,1024]{1,0:T(8,128)(2,1)} %wq_hbm.1, bf16[1024,1024]{1,0:T(8,128)(2,1)} %wk_hbm.1, ...), custom_call_target="tpu_custom_call" | custom-call | flops 16999999488 | bytes 18874368 | tf_op jit(solution)/shard_map/pallas_call | solution.py:346
  30.9 12.0 %shard_map.74 = bf16[2048,1024]{1,0:T(8,128)(2,1)} custom-call(s32[16,128]{1,0:T(8,128)} %bitcast.3, f32[8,128]{1,0:T(8,128)} %get-tuple-element.9.carry_id, f32[1,1024]{1,0:T(1,128)} %bitcast.4, bf16[8,128,128]{2,1,0:T(8,128)(2,1)} %get-tuple-element.10.carry, bf16[2048,1024]{1,0:T(8,128)(2,1)} %get-tuple-element.11.q_ref, ...), custom_call_target="tpu_custom_call" | custom-call | flops 5000000000 | bytes 14680064 | tf_op jit(solution)/shard_map/pallas_call | solution.py:352
